TPU v7x, 256 devices: a whole 4x4x8 slice. The times are simulated.
256 devices in a mesh: rep: 32 (over z, y_lo, core), fsdp: 8 (over y_hi, x).
Axes of the slice: x: 4, y: 4 (y_hi: 2, y_lo: 2; y = y_hi * 2 + y_lo), z: 8, core: 2. Of those that a mesh axis runs over, the one named last changes fastest.
Arguments:
- tokens: bfloat16 [32768, 8192], P(('rep', 'fsdp')), may hold values from -6 to 6
- cotangent: bfloat16 [32768, 8192], P(('rep', 'fsdp')), may hold values from -6 to 6
- weights: bfloat16 [32, 8192, 1536], P('rep', 'fsdp'), may hold values from -6 to 6
- global_params: bfloat16 [8192, 1536], P(('fsdp', 'rep')), may hold values from -12 to 12
- momentum: float32 [8192, 1536], P(('fsdp', 'rep')), may hold values from -2 to 2
- fragment: int32 [1], replicated, may hold values from 0 to 65535
Outputs:
- new_weights: bfloat16 [32, 8192, 1536], P('rep', 'fsdp')
- new_global: bfloat16 [8192, 1536], P(('fsdp', 'rep'))
- new_momentum: float32 [8192, 1536], P(('fsdp', 'rep'))
All inputs are finite; a program needn't handle non-finite values.
Results may differ from a plain program's by a relative error of at most 0.015.
Values may be sent and summed in bfloat16 or wider, within the bound.
A program may use at most 128 MiB of HBM per device.

v0:
```python
import math

import jax
import jax.numpy as jnp
from jax import lax
from jax.experimental import pallas as pl
from jax.experimental.pallas import tpu as pltpu
from jax.sharding import PartitionSpec as P

D = 8192
FRAG = 128
NFRAG = 4
HID = 512
NF = 8
NX = 4
NZ = 8
NQ = 16
ROWS = 128
HALF = ROWS // 2
DEPTH = D // NF
SHARE = 32
WIDE = 3 * FRAG
PAIR = 2 * FRAG
CHUNKS = 4
TILE = 256
PLACE = 512


INNER_RATE = 0.5
OUTER_RATE = 0.7
MOMENT = 0.9
MIX_RATE = 0.5
SCALE_IN = 1.0 / math.sqrt(D)
SCALE_HID = 1.0 / math.sqrt(HID)
BF16 = jnp.bfloat16
F32 = jnp.float32
MESH = pl.DeviceIdType.MESH


def dot(a, b):
    return jnp.dot(a, b, preferred_element_type=F32)


def step_kernel(
    tokens,
    cotangent,
    weights,
    global_ref,
    moment_ref,
    fragment,
    u_out,
    g_out,
    m_out,
    tcut,
    ccut,
    tturn,
    cturn,
    w,
    wrot,
    ysend,
    yrecv,
    far,
    near,
    psend,
    precv,
    prow,
    acts,
    u,
    u0,
    r1,
    s1,
    r2,
    gall,
    local_sem,
    a_send,
    a_recv,
    y_send,
    y_recv,
    h_send,
    h_recv,
    c_send,
    c_recv,
    s_send,
    s_recv,
    g_send,
    g_recv,
    t_send,
    t_recv,
    b_send,
    b_recv,
    entered,
):
    rep = lax.axis_index("rep")
    me = lax.axis_index("fsdp")
    x, yh = me % NX, me // NX
    core, q = rep % 2, rep // 2
    z, yl = q // 2, q % 2
    frag = lax.rem(fragment[0], NFRAG)

    def fsdp_to(k):
        return (x + k % NX) % NX + NX * ((yh + k // NX) % 2)

    def fsdp_from(k):
        return (x + NX - k % NX) % NX + NX * ((yh + k // NX) % 2)

    def q_to(k):
        return ((z + k // 2) % NZ) * 2 + (yl + k % 2) % 2

    def q_from(k):
        return ((z + NZ - k // 2) % NZ) * 2 + (yl + k % 2) % 2

    def at_fsdp(f):
        return (rep, f)

    def at_q(p):
        return (p * 2 + core, me)

    partner = (q * 2 + 1 - core, me)

    def each(n, body):
        def step(k, carry):
            body(k)
            return carry

        lax.fori_loop(0, n, step, 0)

    barrier = pltpu.get_barrier_semaphore()

    def greet_fsdp(i):
        pl.semaphore_signal(barrier, inc=1, device_id=at_fsdp(fsdp_to(i + 1)), device_id_type=MESH)

    def neighbour(dz, dy):
        return at_q((z + dz) % NZ * 2 + (yl + dy) % 2)

    def greet(sem, to):
        pl.semaphore_signal(sem, inc=1, device_id=to, device_id_type=MESH)

    each(NF - 1, greet_fsdp)
    greet(barrier, partner)
    greet(barrier, neighbour(0, 1))
    greet(barrier, neighbour(1, 0))
    greet(barrier, neighbour(NZ - 1, 0))

    own_cols = pl.ds(pl.multiple_of(me * DEPTH, DEPTH), DEPTH)
    own_rows = pl.ds(pl.multiple_of(me * ROWS, ROWS), ROWS)
    load_w = pltpu.make_async_copy(weights.at[0], w, local_sem.at[0])
    load_t = pltpu.make_async_copy(tokens.at[:, own_cols], tcut.at[own_rows], local_sem.at[1])
    load_c = pltpu.make_async_copy(cotangent.at[:, own_cols], ccut.at[own_rows], local_sem.at[2])
    load_w.start()
    load_t.start()
    load_c.start()
    pl.semaphore_wait(barrier, NF - 1 + 4)

    def all_of(block, send, recv):
        return pltpu.make_async_remote_copy(
            src_ref=block,
            dst_ref=block,
            send_sem=send,
            recv_sem=recv,
            device_id=partner,
            device_id_type=MESH,
        )

    others = pl.ds(0, (NF - 1) * ROWS)

    part = ROWS // CHUNKS

    def exchange(source, target, h, slot, k):
        f = fsdp_to(k)
        cols = pl.ds(pl.multiple_of(f * DEPTH, DEPTH), DEPTH)
        rows = pl.ds(pl.multiple_of(me * ROWS + h * part, part), part)
        return pltpu.make_async_remote_copy(
            src_ref=source.at[pl.ds(h * part, part), cols],
            dst_ref=target.at[rows],
            send_sem=a_send.at[slot],
            recv_sem=a_recv.at[slot],
            device_id=at_fsdp(f),
            device_id_type=MESH,
        )

    for h in range(CHUNKS):
        each(NF - 1, lambda i: exchange(tokens, tcut, h, 0, NF - 1 - i).start())
    for h in range(CHUNKS):
        each(NF - 1, lambda i: exchange(cotangent, ccut, h, 1, NF - 1 - i).start())

    for step in range(2):
        greet(entered.at[step], neighbour(1 + step, 0))
        greet(entered.at[step], neighbour(NZ - 1 - step, 0))
        pl.semaphore_wait(entered.at[step], 2)
    greet(entered.at[2], neighbour(0, 1))
    pl.semaphore_wait(entered.at[2], 1)

    load_w.wait()
    for j in range(NFRAG):
        first = lax.rem(frag + j, NFRAG) * FRAG
        for member in range(3):
            cols = pl.ds(first + member * HID, FRAG)
            wrot[j, :, member * FRAG : (member + 1) * FRAG] = w[:, cols]

    def tile_of(i):
        return pl.ds(pl.multiple_of(i * TILE, TILE), TILE)

    def spread(j, i, cols, value):
        block = value.astype(BF16).reshape(TILE // ROWS, ROWS, value.shape[-1])
        ysend[j, i // 2, pl.ds(i % 2 * 2, 2), :, cols] = block

    load_t.wait()
    all_of(tcut.at[others], a_send.at[0], a_recv.at[0]).wait_recv()

    def forward_t(i):
        rows = tcut[tile_of(i), :]
        for j in range(NFRAG):
            spread(j, i, slice(0, PAIR), dot(rows, wrot[j, :, :PAIR]) * SCALE_IN)
        tturn[:, tile_of(i)] = rows.T

    each(NF * ROWS // TILE, forward_t)

    lanes_of = (pl.ds(0, PAIR), pl.ds(PAIR, FRAG))

    def send_terms(k, at):
        f = fsdp_to(k)
        return pltpu.make_async_remote_copy(
            src_ref=ysend.at[0, f // NX, f % NX, :, lanes_of[at]],
            dst_ref=yrecv.at[k, :, lanes_of[at]],
            send_sem=y_send.at[at],
            recv_sem=y_recv.at[at],
            device_id=at_fsdp(f),
            device_id_type=MESH,
        )

    each(NF - 1, lambda i: send_terms(i + 1, 0).start())

    load_c.wait()
    all_of(ccut.at[others], a_send.at[1], a_recv.at[1]).wait_recv()

    def forward_c(groups):
        def run(i):
            rows = ccut[tile_of(i), :]
            for j in groups:
                spread(j, i, slice(PAIR, WIDE), dot(rows, wrot[j, :, PAIR:]) * SCALE_HID)

        return run

    def block_of(j, f):
        return acts.at[j, pl.ds(pl.multiple_of(f * ROWS, ROWS), ROWS)]

    def send_acts(k):
        block = block_of(0, me)
        return pltpu.make_async_remote_copy(
            src_ref=block,
            dst_ref=block,
            send_sem=h_send.at[0],
            recv_sem=h_recv.at[0],
            device_id=at_fsdp(fsdp_to(k)),
            device_id_type=MESH,
        )

    sent_terms = [
        all_of(yrecv.at[pl.ds(1, NF - 1), :, lanes_of[at]], y_send.at[at], y_recv.at[at])
        for at in range(2)
    ]
    sent_acts = all_of(acts.at[0, others], h_send.at[0], h_recv.at[0])

    ahead = ((x + 1) % NX, (x + 3) % NX)
    opposite = (x + 2) % NX
    beside = tuple(at_fsdp(at + NX * yh) for at in ahead)
    pole = at_fsdp(x + NX * (1 - yh))
    halves = (pl.ds(0, HALF), pl.ds(HALF, HALF))
    first_row = (1, 2)
    first_pole = (3,)

    def hop(source, target, sends, recvs, j, slot, to):
        return pltpu.make_async_remote_copy(
            src_ref=source,
            dst_ref=target,
            send_sem=sends.at[0],
            recv_sem=recvs.at[j - 1, slot],
            device_id=to,
            device_id_type=MESH,
        )

    def span_of(j):
        return pl.ds(yh, 1) if j in first_pole else pl.ds(0, 2)

    def seat_of(j):
        return pl.ds(0, 1) if j in first_pole else pl.ds(0, 2)

    def term_far(j, way):
        return hop(
            ysend.at[j, span_of(j), opposite, halves[way]],
            far.at[j - 1, way, seat_of(j)],
            t_send,
            t_recv,
            j,
            way,
            beside[way],
        )

    def term_near(j, way, late):
        half = halves[way if late else 1 - way]
        return hop(
            ysend.at[j, span_of(j), ahead[way], half],
            near.at[j - 1, way, seat_of(j), half],
            t_send,
            t_recv,
            j,
            2,
            beside[way],
        )

    def term_pole(j):
        if j in first_pole:
            return hop(ysend.at[j, 1 - yh], prow, t_send, t_recv, j, 3, pole)
        return hop(psend.at[j - 1], precv.at[j - 1], t_send, t_recv, j, 3, pole)

    def terms_far(j):
        for way in range(2):
            term_far(j, way).start()

    def terms_near(j):
        for way in range(2):
            term_near(j, way, 0).start()

    def terms_row_in(j):
        term_pole(j).wait_recv()
        ysend[j, yh] = (ysend[j, yh].astype(F32) + prow[...].astype(F32)).astype(BF16)

    def terms_pass(j):
        for way in range(2):
            term_far(j, way).wait_recv()
            own = ysend[j, span_of(j), ahead[way], halves[way]].astype(F32)
            sums = own + far[j - 1, way, seat_of(j)].astype(F32)
            ysend[j, span_of(j), ahead[way], halves[way]] = sums.astype(BF16)
            term_near(j, way, 1).start()

    def terms_got(j):
        all_of(near.at[j - 1, :, seat_of(j)], t_send.at[0], t_recv.at[j - 1, 2]).wait_recv()

    def terms_row(j, half, seat):
        total = ysend[j, half, x].astype(F32)
        for way in range(2):
            total = total + near[j - 1, way, seat].astype(F32)
        return total

    def terms_cross(j):
        terms_got(j)
        psend[j - 1] = terms_row(j, 1 - yh, 1 - yh).astype(BF16)
        term_pole(j).start()

    def terms_end(j):
        if j in first_pole:
            terms_got(j)
            activate(j, terms_row(j, yh, 0))
        else:
            term_pole(j).wait_recv()
            activate(j, terms_row(j, yh, yh) + precv[j - 1].astype(F32))

    def act_pole(j, f):
        return hop(block_of(j, f), block_of(j, f), b_send, b_recv, j, 0, pole)

    def act_near(j, way, other, at):
        block = block_of(j, at + NX * (1 - yh if other else yh))
        slot = 1 + way + 2 * other
        return hop(block, block, b_send, b_recv, j, slot, beside[way])

    def act_far(j, way, other, at):
        f = at + NX * (1 - yh if other else yh)
        rows = pl.ds(pl.multiple_of(f * ROWS + way * HALF, HALF), HALF)
        block = acts.at[j, rows]
        return hop(block, block, b_send, b_recv, j, 5, beside[way])

    def acts_begin(j):
        act_pole(j, me).start()
        for way in range(2):
            act_near(j, way, 0, x).start()

    def acts_turn(j):
        act_pole(j, x + NX * (1 - yh)).wait_recv()
        for way in range(2):
            act_near(j, way, 1, x).start()

    def acts_pass(j, other):
        for way in range(2):
            act_near(j, way, other, ahead[1 - way]).wait_recv()
            act_far(j, way, other, ahead[1 - way]).start()

    def acts_all(j, blocks, slot):
        return all_of(acts.at[j, pl.ds(0, blocks * ROWS)], b_send.at[0], b_recv.at[j - 1, slot])

    def acts_across(j):
        for way in range(2):
            act_near(j, way, 0, ahead[1 - way]).wait_recv()
            act_far(j, way, 0, ahead[1 - way]).start()
            act_pole(j, ahead[1 - way] + NX * yh).start()

    def acts_last(j):
        acts_all(j, 1, 5).wait_recv()
        act_pole(j, opposite + NX * yh).start()

    def acts_end(j):
        if j in first_pole:
            acts_all(j, NX, 0).wait_recv()
        else:
            acts_all(j, 2, 5).wait_recv()

    tiles = NF * ROWS // TILE
    each(tiles, forward_c((0,)))
    each(NF - 1, lambda i: send_terms(i + 1, 1).start())
    each(tiles, forward_c((1,)))
    terms_far(1)
    terms_near(1)
    each(tiles, forward_c((3,)))
    term_pole(3).start()
    each(tiles, forward_c((2,)))

    def turn_c(i):
        cturn[:, tile_of(i)] = ccut[tile_of(i), :].T

    each(tiles, turn_c)

    def activate(j, total):
        gate = total[:, :FRAG]
        up = total[:, FRAG:PAIR]
        hidden_grad = total[:, PAIR:]
        sigmoid = jax.nn.sigmoid(gate)
        silu = gate * sigmoid
        acts[j, own_rows, :FRAG] = (
            hidden_grad * up * sigmoid * (1.0 + gate * (1.0 - sigmoid))
        ).astype(BF16)
        acts[j, own_rows, FRAG:PAIR] = (hidden_grad * silu).astype(BF16)
        acts[j, own_rows, PAIR:] = (silu * up).astype(BF16)

    def descend(j, i):
        rows = tile_of(i)
        grad_in = dot(tturn[rows, :], acts[j, :, :PAIR]) * SCALE_IN
        grad_down = dot(cturn[rows, :], acts[j, :, PAIR:]) * SCALE_HID
        left = wrot[j, rows, :PAIR].astype(F32) - INNER_RATE * grad_in
        right = wrot[j, rows, PAIR:].astype(F32) - INNER_RATE * grad_down
        return left.astype(BF16), right.astype(BF16)

    for sent in sent_terms:
        sent.wait_recv()
    total = ysend[0, yh, x].astype(F32)
    for k in range(1, NF):
        total = total + yrecv[k].astype(F32)
    activate(0, total)
    each(NF - 1, lambda i: send_acts(i + 1).start())
    terms_pass(1)
    terms_far(2)
    terms_near(2)
    terms_row_in(3)
    terms_far(3)
    terms_pass(2)
    terms_near(3)
    sent_acts.wait_recv()

    span = TILE // (2 * SHARE)

    def descend_first(i):
        left, right = descend(0, i)
        at = pl.ds(i * span, span)
        u0[at, :, :, :PAIR] = left.reshape(span, 2, SHARE, PAIR)
        u0[at, :, :, PAIR:] = right.reshape(span, 2, SHARE, FRAG)

    each(DEPTH // TILE, descend_first)

    across = pltpu.make_async_remote_copy(
        src_ref=u0.at[:, 1 - core],
        dst_ref=r1,
        send_sem=c_send.at[0],
        recv_sem=c_recv.at[0],
        device_id=partner,
        device_id_type=MESH,
    )
    across.start()

    terms_cross(1)
    terms_pass(3)
    terms_cross(2)

    across.wait()
    s1[...] = (u0[:, core].astype(F32) + r1[...].astype(F32)).astype(BF16)

    def send_sum(k):
        p = q_to(k)
        return pltpu.make_async_remote_copy(
            src_ref=s1.at[p],
            dst_ref=r2.at[k],
            send_sem=s_send.at[0],
            recv_sem=s_recv.at[0],
            device_id=at_q(p),
            device_id_type=MESH,
        )

    each(NQ - 1, lambda i: send_sum(i + 1).start())
    for j in first_row + first_pole:
        terms_end(j)
        acts_begin(j)
    sent_sums = all_of(r2.at[pl.ds(1, NQ - 1)], s_send.at[0], s_recv.at[0])
    sent_sums.wait_recv()

    total = s1[q].astype(F32)
    for k in range(1, NQ):
        total = total + r2[k].astype(F32)
    first = frag * FRAG
    for member in range(3):
        cols = pl.ds(first + member * HID, FRAG)
        lanes = slice(member * FRAG, (member + 1) * FRAG)
        old = global_ref[:, cols].astype(F32)
        average = old - total[:, lanes] / (2 * NQ)
        moment = MOMENT * moment_ref[:, cols] + average
        m_out[:, lanes] = moment
        gall[q, core, :, lanes] = (old - OUTER_RATE * (average + MOMENT * moment)).astype(BF16)
    g_out[...] = gall[q, core]

    def send_global(k):
        block = gall.at[q, core]
        return pltpu.make_async_remote_copy(
            src_ref=block,
            dst_ref=block,
            send_sem=g_send.at[0],
            recv_sem=g_recv.at[0],
            device_id=at_q(q_to(k)),
            device_id_type=MESH,
        )

    sent_global = all_of(gall.at[pl.ds(0, NQ - 1), core], g_send.at[0], g_recv.at[0])
    each(NQ - 1, lambda i: send_global(i + 1).start())

    for j in first_row:
        acts_turn(j)
    for j in first_pole:
        acts_across(j)
    for j in first_row:
        acts_pass(j, 0)
    for j in first_pole:
        acts_last(j)
    for j in first_row:
        acts_pass(j, 1)

    def descend_rest(j):
        def run(i):
            left, right = descend(j, i)
            u[j, tile_of(i), :PAIR] = left
            u[j, tile_of(i), PAIR:] = right

        return run

    def store(j):
        return pltpu.make_async_copy(u.at[j], u_out.at[j], local_sem.at[3 + j])

    sent_global.wait_recv()
    side = gall.at[:, core]
    give = pltpu.make_async_remote_copy(
        src_ref=side,
        dst_ref=side,
        send_sem=c_send.at[1],
        recv_sem=c_recv.at[1],
        device_id=partner,
        device_id_type=MESH,
    )
    give.start()

    def finish(j):
        acts_end(j)
        each(DEPTH // TILE, descend_rest(j))
        store(j).start()

    finish(1)
    finish(2)
    give.wait_send()
    other = gall.at[:, 1 - core]
    pltpu.make_async_remote_copy(
        src_ref=other,
        dst_ref=other,
        send_sem=c_send.at[1],
        recv_sem=c_recv.at[1],
        device_id=partner,
        device_id_type=MESH,
    ).wait_recv()

    def mix(i):
        at = pl.ds(i * span, span)
        mixed = MIX_RATE * u0[at].astype(F32) + (1.0 - MIX_RATE) * gall[at].astype(F32)
        u[0, tile_of(i), :] = mixed.astype(BF16).reshape(TILE, WIDE)

    each(DEPTH // TILE, mix)
    store(0).start()
    finish(3)

    all_of(tcut.at[others], a_send.at[0], a_recv.at[0]).wait_send()
    all_of(ccut.at[others], a_send.at[1], a_recv.at[1]).wait_send()
    for sent in sent_terms:
        sent.wait_send()
    sent_acts.wait_send()
    every = acts.at[pl.ds(0, NFRAG - 1), others]
    all_of(every, t_send.at[0], t_recv.at[0, 0]).wait_send()
    all_of(every, b_send.at[0], b_recv.at[0, 0]).wait_send()
    sent_sums.wait_send()
    sent_global.wait_send()

    for j in range(NFRAG):
        store(j).wait()


def place_kernel(u, g, m, global_ref, moment_ref, fragment, w_out, g_out, m_out):
    frag = lax.rem(fragment[0], NFRAG)
    for at in range(NFRAG):
        j = lax.rem(at + NFRAG - frag, NFRAG)
        for member in range(3):
            cols = slice(member * HID + at * FRAG, member * HID + (at + 1) * FRAG)
            w_out[0, :, cols] = u[j, :, member * FRAG : (member + 1) * FRAG]

    @pl.when(pl.program_id(0) == 0)
    def _():
        for at in range(NFRAG):
            here = frag == at
            for member in range(3):
                cols = slice(member * HID + at * FRAG, member * HID + (at + 1) * FRAG)
                lanes = slice(member * FRAG, (member + 1) * FRAG)
                g_out[:, cols] = jnp.where(here, g[:, lanes], global_ref[:, cols])
                m_out[:, cols] = jnp.where(here, m[:, lanes], moment_ref[:, cols])


def shards(tokens, cotangent, weights, global_params, momentum, fragment):
    anywhere = pl.BlockSpec(memory_space=pl.ANY)
    vmem = pl.BlockSpec(memory_space=pltpu.VMEM)
    smem = pl.BlockSpec(memory_space=pltpu.SMEM)
    sem = pltpu.SemaphoreType.DMA
    u, g, m = pl.pallas_call(
        step_kernel,
        out_shape=(
            jax.ShapeDtypeStruct((NFRAG, DEPTH, WIDE), BF16),
            jax.ShapeDtypeStruct((SHARE, WIDE), BF16),
            jax.ShapeDtypeStruct((SHARE, WIDE), F32),
        ),
        in_specs=[anywhere, anywhere, anywhere, vmem, vmem, smem],
        out_specs=(anywhere, vmem, vmem),
        scratch_shapes=[
            pltpu.VMEM((NF * ROWS, DEPTH), BF16),
            pltpu.VMEM((NF * ROWS, DEPTH), BF16),
            pltpu.VMEM((DEPTH, NF * ROWS), BF16),
            pltpu.VMEM((DEPTH, NF * ROWS), BF16),
            pltpu.VMEM((DEPTH, 3 * HID), BF16),
            pltpu.VMEM((NFRAG, DEPTH, WIDE), BF16),
            pltpu.VMEM((NFRAG, 2, NX, ROWS, WIDE), BF16),
            pltpu.VMEM((NF, ROWS, WIDE), BF16),
            pltpu.VMEM((NFRAG - 1, 2, 2, HALF, WIDE), BF16),
            pltpu.VMEM((NFRAG - 1, 2, 2, ROWS, WIDE), BF16),
            pltpu.VMEM((NFRAG - 1, ROWS, WIDE), BF16),
            pltpu.VMEM((NFRAG - 1, ROWS, WIDE), BF16),
            pltpu.VMEM((NX, ROWS, WIDE), BF16),
            pltpu.VMEM((NFRAG, NF * ROWS, WIDE), BF16),
            pltpu.VMEM((NFRAG, DEPTH, WIDE), BF16),
            pltpu.VMEM((NQ, 2, SHARE, WIDE), BF16),
            pltpu.VMEM((NQ, SHARE, WIDE), BF16),
            pltpu.VMEM((NQ, SHARE, WIDE), BF16),
            pltpu.VMEM((NQ, SHARE, WIDE), BF16),
            pltpu.VMEM((NQ, 2, SHARE, WIDE), BF16),
            sem((3 + NFRAG,)),
            sem((2,)),
            sem((2,)),
            sem((2,)),
            sem((2,)),
            sem((1,)),
            sem((1,)),
            sem((2,)),
            sem((2,)),
            sem((1,)),
            sem((1,)),
            sem((1,)),
            sem((1,)),
            sem((1,)),
            sem((NFRAG - 1, 4)),
            sem((1,)),
            sem((NFRAG - 1, 6)),
            pltpu.SemaphoreType.REGULAR((3,)),
        ],
        compiler_params=pltpu.CompilerParams(
            collective_id=0, has_side_effects=True, vmem_limit_bytes=56 * 2**20
        ),
        cost_estimate=pl.CostEstimate(
            flops=4 * ROWS * D * 3 * HID, bytes_accessed=10 * 2**20, transcendentals=ROWS * HID
        ),
    )(tokens, cotangent, weights, global_params, momentum, fragment)
    return pl.pallas_call(
        place_kernel,
        out_shape=(
            jax.ShapeDtypeStruct((1, DEPTH, 3 * HID), BF16),
            jax.ShapeDtypeStruct(global_params.shape, BF16),
            jax.ShapeDtypeStruct(momentum.shape, F32),
        ),
        grid=(DEPTH // PLACE,),
        in_specs=[
            pl.BlockSpec((NFRAG, PLACE, WIDE), lambda i: (0, i, 0)),
            vmem,
            vmem,
            vmem,
            vmem,
            smem,
        ],
        out_specs=(pl.BlockSpec((1, PLACE, 3 * HID), lambda i: (0, i, 0)), vmem, vmem),
        cost_estimate=pl.CostEstimate(flops=0, bytes_accessed=6 * 2**20, transcendentals=0),
    )(u, g, m, global_params, momentum, fragment)


def solution(mesh):
    placed = (
        P(("rep", "fsdp"), None),
        P(("rep", "fsdp"), None),
        P("rep", "fsdp", None),
        P(("fsdp", "rep"), None),
        P(("fsdp", "rep"), None),
        P(),
    )
    return jax.shard_map(
        shards,
        mesh=mesh,
        in_specs=placed,
        out_specs=(P("rep", "fsdp", None), P(("fsdp", "rep"), None), P(("fsdp", "rep"), None)),
        check_vma=False,
    )
```

profile of v0, /device:TPU:16, one launch (start us, length us, event | category | flops | bytes accessed | tf_op | source)
XLA Modules:
  0.0 125.1 jit_solution(6811554936612619558)
XLA Ops:
  1.3 120.3 %shard_map.85 = (bf16[4,1024,384]{2,1,0:T(8,128)(2,1)}, bf16[32,384]{1,0:T(8,128)(2,1)}, f32[32,384]{1,0:T(8,128)}) custom-call(bf16[128,8192]{1,0:T(8,128)(2,1)} %tokens.1, bf16[128,8192]{1,0:T(8,128)(2,1)} %cotangent.1, bf16[1,1024,1536]{2,1,0:T(8,128)(2,1)} %weights.1, bf16[32,1536]{1,0:T(8,128)(2,1)} %global_ref.3, f32[32,1536]{1,0:T(8,128)} %moment_ref.3, ...), custom_call_target="tpu_custom_call" | custom-call | flops 6442450944 | bytes 10485760 | tf_op jit(solution)/shard_map/pallas_call | solution.py:630
  121.5 3.5 %shard_map.86 = (bf16[1,1024,1536]{2,1,0:T(8,128)(2,1)}, bf16[32,1536]{1,0:T(8,128)(2,1)}, f32[32,1536]{1,0:T(8,128)}) custom-call(bf16[4,1024,384]{2,1,0:T(8,128)(2,1)} %get-tuple-element.6.u, bf16[32,384]{1,0:T(8,128)(2,1)} %get-tuple-element.7.g, f32[32,384]{1,0:T(8,128)} %get-tuple-element.8.m, bf16[32,1536]{1,0:T(8,128)(2,1)} %global_ref.3, ...), custom_call_target="tpu_custom_call" | custom-call | bytes 6291456 | tf_op jit(solution)/shard_map/pallas_call | solution.py:686
where the time goes:
time: 125 us
  Pallas kernels  124 us (99%)
  between operations  1.29 us (1%)
    pallas_call x1, Pallas kernels, shards(): pl.pallas_call(step_kernel, out_shape=(jax.ShapeDtypeStruct((NFRAG, DEPTH...  120 us
    pallas_call x1, Pallas kernels, shards(): pl.pallas_call(place_kernel, out_shape=(jax.ShapeDtypeStruct((1, DEPTH, 3...  3.55 us

commit v1 on v0

--- a/solution.py
+++ b/solution.py
@@ -126,16 +126,15 @@
 
     barrier = pltpu.get_barrier_semaphore()
 
-    def greet_fsdp(i):
-        pl.semaphore_signal(barrier, inc=1, device_id=at_fsdp(fsdp_to(i + 1)), device_id_type=MESH)
-
     def neighbour(dz, dy):
         return at_q((z + dz) % NZ * 2 + (yl + dy) % 2)
 
     def greet(sem, to):
         pl.semaphore_signal(sem, inc=1, device_id=to, device_id_type=MESH)
 
-    each(NF - 1, greet_fsdp)
+    nearest = [at_fsdp(fsdp_to(k)) for k in (1, 3, 4)]
+    for to in nearest:
+        greet(barrier, to)
     greet(barrier, partner)
     greet(barrier, neighbour(0, 1))
     greet(barrier, neighbour(1, 0))
@@ -149,7 +148,7 @@
     load_w.start()
     load_t.start()
     load_c.start()
-    pl.semaphore_wait(barrier, NF - 1 + 4)
+    pl.semaphore_wait(barrier, 3 + 4)
 
     def all_of(block, send, recv):
         return pltpu.make_async_remote_copy(
@@ -178,7 +177,17 @@
             device_id_type=MESH,
         )
 
-    for h in range(CHUNKS):
+    for k in (4, 1, 3):
+        exchange(tokens, tcut, 0, 0, k).start()
+    for to in nearest:
+        greet(entered.at[3], to)
+    pl.semaphore_wait(entered.at[3], 3)
+    greet(entered.at[4], nearest[1])
+    for k in (5, 7, 2):
+        exchange(tokens, tcut, 0, 0, k).start()
+    pl.semaphore_wait(entered.at[4], 1)
+    exchange(tokens, tcut, 0, 0, 6).start()
+    for h in range(1, CHUNKS):
         each(NF - 1, lambda i: exchange(tokens, tcut, h, 0, NF - 1 - i).start())
     for h in range(CHUNKS):
         each(NF - 1, lambda i: exchange(cotangent, ccut, h, 1, NF - 1 - i).start())
@@ -405,7 +414,8 @@
 
     tiles = NF * ROWS // TILE
     each(tiles, forward_c((0,)))
-    each(NF - 1, lambda i: send_terms(i + 1, 1).start())
+    for k in range(NF - 1, 0, -1):
+        send_terms(k, 1).start()
     each(tiles, forward_c((1,)))
     terms_far(1)
     terms_near(1)
@@ -444,7 +454,8 @@
     for k in range(1, NF):
         total = total + yrecv[k].astype(F32)
     activate(0, total)
-    each(NF - 1, lambda i: send_acts(i + 1).start())
+    for k in range(NF - 1, 0, -1):
+        send_acts(k).start()
     terms_pass(1)
     terms_far(2)
     terms_near(2)
@@ -475,11 +486,10 @@
     across.start()
 
     terms_cross(1)
-    terms_pass(3)
-    terms_cross(2)
-
     across.wait()
     s1[...] = (u0[:, core].astype(F32) + r1[...].astype(F32)).astype(BF16)
+
+    far_first = (8, 9, 7, 11, 6, 10, 5, 13, 4, 12, 3, 15, 2, 14, 1)
 
     def send_sum(k):
         p = q_to(k)
@@ -492,7 +502,11 @@
             device_id_type=MESH,
         )
 
-    each(NQ - 1, lambda i: send_sum(i + 1).start())
+    for k in far_first:
+        send_sum(k).start()
+    terms_pass(3)
+    terms_cross(2)
+
     for j in first_row + first_pole:
         terms_end(j)
         acts_begin(j)
@@ -525,7 +539,8 @@
         )
 
     sent_global = all_of(gall.at[pl.ds(0, NQ - 1), core], g_send.at[0], g_recv.at[0])
-    each(NQ - 1, lambda i: send_global(i + 1).start())
+    for k in far_first:
+        send_global(k).start()
 
     for j in first_row:
         acts_turn(j)
@@ -674,7 +689,7 @@
             sem((NFRAG - 1, 4)),
             sem((1,)),
             sem((NFRAG - 1, 6)),
-            pltpu.SemaphoreType.REGULAR((3,)),
+            pltpu.SemaphoreType.REGULAR((5,)),
         ],
         compiler_params=pltpu.CompilerParams(
             collective_id=0, has_side_effects=True, vmem_limit_bytes=56 * 2**20

time: 125 us -> 123 us (0.984)
  Pallas kernels: 124 us -> 121 us
    pallas_call x1, Pallas kernels: 120 us -> 118 us  [shards(): pl.pallas_call(step_kernel, out_shape=(jax.ShapeDtypeStruct((NFRAG, DEPTH...]
where the time goes in v1:
time: 123 us; the launch traced here: 122 us
  Pallas kernels  121 us (98%)
  between operations  1.29 us (1%)
    pallas_call x1, Pallas kernels, shards(): pl.pallas_call(step_kernel, out_shape=(jax.ShapeDtypeStruct((NFRAG, DEPTH...  118 us
    pallas_call x1, Pallas kernels, shards(): pl.pallas_call(place_kernel, out_shape=(jax.ShapeDtypeStruct((1, DEPTH, 3...  3.55 us

profile of v1, /device:TPU:16, one launch (start us, length us, event | category | flops | bytes accessed | tf_op | source)
XLA Modules:
  0.0 122.4 jit_solution(8547010811681332188)
XLA Ops:
  1.3 117.6 %shard_map.85 = (bf16[4,1024,384]{2,1,0:T(8,128)(2,1)}, bf16[32,384]{1,0:T(8,128)(2,1)}, f32[32,384]{1,0:T(8,128)}) custom-call(bf16[128,8192]{1,0:T(8,128)(2,1)} %tokens.1, bf16[128,8192]{1,0:T(8,128)(2,1)} %cotangent.1, bf16[1,1024,1536]{2,1,0:T(8,128)(2,1)} %weights.1, bf16[32,1536]{1,0:T(8,128)(2,1)} %global_ref.3, f32[32,1536]{1,0:T(8,128)} %moment_ref.3, ...), custom_call_target="tpu_custom_call" | custom-call | flops 6442450944 | bytes 10485760 | tf_op jit(solution)/shard_map/pallas_call | solution.py:645
  118.8 3.5 %shard_map.86 = (bf16[1,1024,1536]{2,1,0:T(8,128)(2,1)}, bf16[32,1536]{1,0:T(8,128)(2,1)}, f32[32,1536]{1,0:T(8,128)}) custom-call(bf16[4,1024,384]{2,1,0:T(8,128)(2,1)} %get-tuple-element.6.u, bf16[32,384]{1,0:T(8,128)(2,1)} %get-tuple-element.7.g, f32[32,384]{1,0:T(8,128)} %get-tuple-element.8.m, bf16[32,1536]{1,0:T(8,128)(2,1)} %global_ref.3, ...), custom_call_target="tpu_custom_call" | custom-call | bytes 6291456 | tf_op jit(solution)/shard_map/pallas_call | solution.py:701
